TPU v7x, 512 devices: a whole 4x4x16 slice. The times are simulated.
512 devices in a mesh: dp: 16 (over y, x), expert: 32 (over z, core).
Axes of the slice: x: 4, y: 4, z: 16, core: 2. Of those that a mesh axis runs over, the one named last changes fastest.
Arguments:
- tokens: bfloat16 [65536, 512], P(('dp', 'expert')), may hold values from -6 to 6
- cotangent: bfloat16 [65536, 512], P(('dp', 'expert')), may hold values from -0.29882812 to 0.29882812
- labels: int32 [65536, 1], P(('dp', 'expert')), may hold values from 0 to 63; in each aligned block of 128 rows (0 to 127, 128 to 255, ...) at most 4 rows name the same one
- placement: int32 [64], replicated, may hold values from 0 to 63, each once
- mass: float32 [65536], P(('dp', 'expert')), may hold values from 0.1 to 10
- w_head: float32 [512, 16], replicated, may hold values from -0.25 to 0.25
- w_up: bfloat16 [64, 512, 2048], P('expert', None, 'dp'), may hold values from -0.25 to 0.25
- w_down: bfloat16 [64, 2048, 512], P('expert', 'dp'), may hold values from -0.125 to 0.125
- up_moment: bfloat16 [64, 512, 2048], P('expert', None, 'dp'), may hold values from -2 to 2
- up_square: bfloat16 [64, 512, 2048], P('expert', None, 'dp'), may hold values from 0.0099487305 to 1
- down_moment: bfloat16 [64, 2048, 512], P('expert', 'dp'), may hold values from -2 to 2
- down_square: bfloat16 [64, 2048, 512], P('expert', 'dp'), may hold values from 0.0099487305 to 1
Outputs:
- fine_precip: float32 [65536, 16], P(('dp', 'expert'))
- up_next: bfloat16 [64, 512, 2048], P('expert', None, 'dp')
- down_next: bfloat16 [64, 2048, 512], P('expert', 'dp')
- up_moment_next: bfloat16 [64, 512, 2048], P('expert', None, 'dp')
- up_square_next: bfloat16 [64, 512, 2048], P('expert', None, 'dp')
- down_moment_next: bfloat16 [64, 2048, 512], P('expert', 'dp')
- down_square_next: bfloat16 [64, 2048, 512], P('expert', 'dp')
Inputs may be any that keep to these rules, and one draw needn't show every extreme that they name: `labels`: within each device's block of 128 rows no regime is named more than 4 times, and in every draw some regime is named exactly 4 times in some block; every regime is named somewhere. `placement`: each regime stands in exactly one expert slot.
All inputs are finite; a program needn't handle non-finite values.
Results may differ from a plain program's by a relative error of at most 0.0045.
Values may be sent and summed in bfloat16 or wider, within the bound.
A program may use at most 64 MiB of HBM per device.

v0:
```python
import jax
import jax.numpy as jnp
from jax import lax
from jax.sharding import PartitionSpec as P

CAP = 4
beta_first = 0.9
beta_second = 0.95
correct_first = 1.0 - 0.9**20
correct_second = 1.0 - 0.95**20
learn_rate = 0.002
adam_epsilon = 1e-08


def gelu_parts(pre):
    normal_cdf = 0.5 * (1.0 + lax.erf(pre * 0.7071067811865476))
    density = jnp.exp(-0.5 * pre * pre) * 0.3989422804014327
    return (pre * normal_cdf, normal_cdf + pre * density)


def adam_step(weight, first, second, grad):
    new_first = beta_first * first.astype(jnp.float32) + (1.0 - beta_first) * grad
    new_second = beta_second * second.astype(jnp.float32) + (1.0 - beta_second) * grad * grad
    update = new_first / correct_first / (jnp.sqrt(new_second / correct_second) + adam_epsilon)
    moved = weight.astype(jnp.float32) - learn_rate * update
    return (
        moved.astype(jnp.bfloat16),
        new_first.astype(jnp.bfloat16),
        new_second.astype(jnp.bfloat16),
    )


def route_slots(labels, placement, capacity, holders, local_count):
    experts = placement.shape[0]
    regimes = jnp.arange(experts, dtype=jnp.int32)
    owner = jnp.sum(jnp.where(placement[None, :] == regimes[:, None], regimes[None, :], 0), axis=1)
    chosen = labels[:, 0][:, None] == regimes[None, :]
    target = jnp.sum(jnp.where(chosen, owner[None, :], 0), axis=1)
    onehot = (target[:, None] == regimes[None, :]).astype(jnp.int32)
    earlier = jnp.cumsum(onehot, axis=0) - onehot
    position = jnp.sum(earlier * onehot, axis=1)
    lane_index = target % local_count * holders + target // local_count
    return lane_index * capacity + position


def fill_slots(values, slots, count):
    row_count = values.shape[0]
    source = (
        jnp.full((count,), row_count, jnp.int32)
        .at[slots]
        .set(jnp.arange(row_count, dtype=jnp.int32))
    )
    padded = jnp.concatenate([values, jnp.zeros((1, values.shape[1]), values.dtype)], axis=0)
    return jnp.take(padded, source, axis=0)


def expert_rows(rows_x, rows_grad, w_in, w_out):
    pre = jnp.einsum("krd,kdf->krf", rows_x, w_in, preferred_element_type=jnp.float32)
    value, slope = gelu_parts(pre)
    hidden = value.astype(jnp.bfloat16)
    back = jnp.einsum("krd,kfd->krf", rows_grad, w_out, preferred_element_type=jnp.float32)
    hidden_grad = (back * slope).astype(jnp.bfloat16)
    return (hidden, hidden_grad)


def outer_in(rows_x, hidden_grad):
    return jnp.einsum("krd,krf->kdf", rows_x, hidden_grad, preferred_element_type=jnp.float32)


def outer_out(hidden, rows_grad):
    return jnp.einsum("krf,krd->kfd", hidden, rows_grad, preferred_element_type=jnp.float32)


def local(
    tokens,
    cotangent,
    labels,
    placement,
    mass,
    w_head,
    w_up,
    w_down,
    up_moment,
    up_square,
    down_moment,
    down_square,
):
    capacity = CAP
    experts = placement.shape[0]
    width = tokens.shape[1]
    local_count = w_up.shape[0]
    holders = lax.axis_size("expert")
    slots = route_slots(labels, placement, capacity, holders, local_count)
    slot_count = experts * capacity
    recv_rows = holders * capacity
    send_x = fill_slots(tokens, slots, slot_count).reshape(local_count, holders, capacity, width)
    send_grad = fill_slots(cotangent, slots, slot_count).reshape(
        local_count, holders, capacity, width
    )
    recv_x, recv_grad = (
        lax.all_to_all(send_x, "expert", split_axis=1, concat_axis=1, tiled=True),
        lax.all_to_all(send_grad, "expert", split_axis=1, concat_axis=1, tiled=True),
    )
    recv_x = recv_x.reshape(local_count, recv_rows, width)
    recv_grad = recv_grad.reshape(local_count, recv_rows, width)
    piece_x = lax.all_gather(recv_x, "dp", axis=1, tiled=True)
    piece_grad = lax.all_gather(recv_grad, "dp", axis=1, tiled=True)
    hidden, hidden_grad = expert_rows(piece_x, piece_grad, w_up, w_down)
    grad_in = outer_in(piece_x, hidden_grad)
    grad_out = outer_out(hidden, piece_grad)
    absorb_hidden_all = jnp.swapaxes(hidden, 0, 1)
    hidden_all, grad_in, grad_out = (absorb_hidden_all, grad_in, grad_out)
    summed = lax.psum_scatter(
        jnp.einsum("rkf,kfd->rkd", hidden_all, w_down, preferred_element_type=jnp.float32).astype(
            jnp.bfloat16
        ),
        "dp",
        scatter_dimension=0,
        tiled=True,
    )
    outgoing = jnp.swapaxes(summed, 0, 1).reshape(local_count, holders, capacity, width)
    returned = lax.all_to_all(outgoing, "expert", split_axis=1, concat_axis=1, tiled=True)
    expert_out = jnp.take(returned.reshape(slot_count, width), slots, axis=0)
    field = tokens.astype(jnp.float32) + expert_out.astype(jnp.float32)
    logits = jnp.dot(
        field, w_head, precision=lax.Precision.HIGHEST, preferred_element_type=jnp.float32
    )
    positive = jax.nn.softplus(logits) + 0.1
    fine_precip = mass[:, None] * positive / jnp.sum(positive, axis=1, keepdims=True)
    up_next, up_moment_next, up_square_next = adam_step(w_up, up_moment, up_square, grad_in)
    down_next, down_moment_next, down_square_next = adam_step(
        w_down, down_moment, down_square, grad_out
    )
    return (
        fine_precip,
        up_next,
        down_next,
        up_moment_next,
        up_square_next,
        down_moment_next,
        down_square_next,
    )


def solution(mesh):
    placed = (
        P(("dp", "expert"), None),
        P(("dp", "expert"), None),
        P(("dp", "expert"), None),
        P(),
        P(("dp", "expert")),
        P(),
        P("expert", None, "dp"),
        P("expert", "dp", None),
        P("expert", None, "dp"),
        P("expert", None, "dp"),
        P("expert", "dp", None),
        P("expert", "dp", None),
    )
    return jax.shard_map(
        local,
        mesh=mesh,
        in_specs=placed,
        out_specs=(
            P(("dp", "expert"), None),
            P("expert", None, "dp"),
            P("expert", "dp", None),
            P("expert", None, "dp"),
            P("expert", None, "dp"),
            P("expert", "dp", None),
            P("expert", "dp", None),
        ),
        check_vma=False,
    )
```

profile of v0, /device:TPU:1, one launch (start us, length us, event | category | flops | bytes accessed | tf_op | source)
XLA Modules:
  0.0 303.4 jit_solution(4484119608090613356)
XLA Ops:
  7.2 0.0 copy-start
  7.2 0.0 all-gather.3.cloned.1.call-start
  7.2 0.8 select_reduce_fusion.2
  8.0 0.8 select_reduce_fusion.1
  8.8 0.1 fusion.28
  8.9 0.2 reduce_window_sum.11
  9.1 0.2 select_reduce_fusion
  9.3 1.0 scatter_custom_fusion
  10.3 0.9 concatenate.7
  11.3 0.9 concatenate.6
  12.2 1.2 gather_fusion.2
  13.3 1.2 gather_fusion.1
  14.5 0.0 copy-start.2
  14.5 0.1 broadcast_select_fusion
  14.6 0.1 reshape.141
  14.7 0.1 copy.29
  14.8 38.5 %all_to_all.15 = bf16[2,32,4,512]{3,2,0,1:T(4,128)(2,1)S(1)} all-to-all(bf16[2,32,4,512]{3,2,0,1:T(4,128)(2,1)S(1)} %copy.29), channel_id=1, replica_groups=mesh['dp'=16,'expert'=32] {'expert'}, dimensions={1} | all-to-all | bytes 524288 | tf_op jit(solution)/shard_map/all_to_all | solution.py:101
  53.3 0.1 copy.30
  53.4 0.8 reshape.142
  54.2 0.0 all-gather.3.cloned.1.call-update
  54.2 0.0 copy-start.1
  54.2 0.0 reduce-scatter.2.cloned.1.call-start
  54.3 58.6 %all-gather.3.cloned.1.call-done = bf16[2,2048,512]{2,1,0:T(8,128)(2,1)} async-done(((bf16[2,128,512]{2,1,0:T(8,128)(2,1)}), bf16[2,2048,512]{2,1,0:T(8,128)(2,1)}) %all-gather.3.cloned.1.call-update) | async-done | bytes 4194320 | tf_op jit(solution)/shard_map/all_gather | solution.py:106
  112.9 3.4 %fusion.46 = f32[2,2048,128]{2,1,0:T(8,128)S(1)} fusion(bf16[2,2048,512]{2,1,0:T(8,128)(2,1)} %all-gather.3.cloned.1.call-done, bf16[2,512,128]{2,1,0:T(8,128)(2,1)S(1)} %copy-done.2), kind=kOutput, calls=%fused_computation.89 | convolution fusion | flops 536870912 | bytes 6553600 | tf_op jit(solution)/shard_map/krd,kdf->krf/dot_general | solution.py:58
  116.4 3.2 %convert_bitcast_fusion = bf16[2048,2,512]{2,0,1:T(8,128)(2,1)} fusion(bf16[2,128,512]{2,1,0:T(8,128)(2,1)S(1)} %copy-done.1, f32[2,2048,128]{2,1,0:T(8,128)S(1)} %fusion.46), kind=kOutput, calls=%fused_computation.4 | convolution fusion | flops 541589504 | bytes 6553600 | tf_op jit(solution)/shard_map/rkf,kfd->rkd/dot_general | solution.py:114
  119.6 0.0 reduce-scatter.2.cloned.1.call-update
  119.6 0.0 all-gather.5.cloned.1.call-start
  119.6 0.1 reshape.145
  119.7 0.0 copy-start.5
  119.7 0.0 copy-start.6
  119.7 0.1 copy.33
  119.8 34.9 %all_to_all.16 = bf16[2,32,4,512]{3,2,0,1:T(4,128)(2,1)S(1)} all-to-all(bf16[2,32,4,512]{3,2,0,1:T(4,128)(2,1)S(1)} %copy.33), channel_id=1, replica_groups=mesh['dp'=16,'expert'=32] {'expert'}, dimensions={1} | all-to-all | bytes 524288 | tf_op jit(solution)/shard_map/all_to_all | solution.py:102
  154.8 0.1 copy.34
  154.9 0.8 reshape.146
  155.6 0.0 all-gather.5.cloned.1.call-update
  155.7 55.1 %reduce-scatter.2.cloned.1.call-done = bf16[128,2,512]{2,0,1:T(8,128)(2,1)} async-done(((bf16[2048,2,512]{2,0,1:T(8,128)(2,1)}), bf16[128,2,512]{2,0,1:T(8,128)(2,1)}) %reduce-scatter.2.cloned.1.call-update) | async-done | bytes 262160 | tf_op jit(solution)/shard_map/reduce_scatter | solution.py:113
  210.8 1.0 reshape.143
  211.8 0.8 copy.31
  212.6 14.6 %all-to-all-start.1 = ((bf16[2,32,4,512]{3,2,0,1:T(4,128)(2,1)}), bf16[2,32,4,512]{3,2,0,1:T(4,128)(2,1)S(1)}, u32[]{:S(2)}, u32[]{:S(2)}) async-start(bf16[2,32,4,512]{3,2,0,1:T(4,128)(2,1)} %copy.31), calls=%async_computation.2 | async-start | bytes 524288 | tf_op jit(solution)/shard_map/all_to_all | solution.py:122
  227.3 55.6 %all-gather.5.cloned.1.call-done = bf16[2,2048,512]{2,1,0:T(8,128)(2,1)} async-done(((bf16[2,128,512]{2,1,0:T(8,128)(2,1)}), bf16[2,2048,512]{2,1,0:T(8,128)(2,1)}) %all-gather.5.cloned.1.call-update) | async-done | bytes 4194320 | tf_op jit(solution)/shard_map/all_gather | solution.py:107
  282.9 4.4 %fusion.19 = (bf16[2,128,512]{2,1,0:T(8,128)(2,1)}, bf16[2,128,512]{2,1,0:T(8,128)(2,1)}, bf16[2,128,512]{2,1,0:T(8,128)(2,1)}) fusion(bf16[2,128,512]{2,1,0:T(8,128)(2,1)S(1)} %copy-done.5, bf16[2,128,512]{2,1,0:T(8,128)(2,1)S(1)} %copy-done.6, bf16[2,128,512]{2,1,0:T(8,128)(2,1)S(1)} %copy-done.1, bf16[2,2048,512]{2,1,0:T(8,128)(2,1)} %all-gather.5.cloned.1.call-done, ...), kind=kOutput, calls=%fused_computation.35 | convolution fusion | flops 541982720 | bytes 7864320 | tf_op jit(solution)/shard_map/krf,krd->kfd/dot_general | solution.py:71
  287.3 7.5 %fusion.20 = (bf16[2,512,128]{2,1,0:T(8,128)(2,1)}, bf16[2,512,128]{2,1,0:T(8,128)(2,1)}, bf16[2,512,128]{2,1,0:T(8,128)(2,1)}) fusion(bf16[2,512,128]{2,1,0:T(8,128)(2,1)} %param.23, bf16[2,512,128]{2,1,0:T(8,128)(2,1)} %param.22, bf16[2,512,128]{2,1,0:T(8,128)(2,1)S(1)} %copy-done.2, bf16[2,2048,512]{2,1,0:T(8,128)(2,1)} %all-gather.3.cloned.1.call-done, ...), kind=kOutput, calls=%fused_computation.36 | convolution fusion | flops 1081475072 | bytes 12320768 | tf_op jit(solution)/shard_map/krd,krf->kdf/dot_general | solution.py:67
  294.7 0.0 all-to-all-done.1
  294.7 0.1 copy.32
  294.8 0.1 reshape.144
  294.9 0.8 gather_fusion
  295.8 0.5 fusion.45
  296.2 0.6 multiply_divide_fusion
  (16 shorter events, 0.1 us)
Async XLA Ops:
  7.2 288.6 %copy-start = (f32[512,16]{0,1:T(8,128)S(1)}, f32[512,16]{0,1:T(8,128)}, u32[]{:S(2)}) copy-start(f32[512,16]{0,1:T(8,128)} %param.19) | copy-start | bytes 98308
  7.2 105.7 %all-gather.3.cloned.1.call-start = ((), (), s32[]{:S(2)}) async-start(), calls=%async_computation.4 | async-start | bytes 4456448 | tf_op jit(solution)/shard_map/all_gather | solution.py:106
  14.5 98.4 %copy-start.2 = (bf16[2,512,128]{2,1,0:T(8,128)(2,1)S(1)}, bf16[2,512,128]{2,1,0:T(8,128)(2,1)}, u32[]{:S(2)}) copy-start(bf16[2,512,128]{2,1,0:T(8,128)(2,1)} %param.20) | copy-start | bytes 786436
  54.2 62.1 %copy-start.1 = (bf16[2,128,512]{2,1,0:T(8,128)(2,1)S(1)}, bf16[2,128,512]{2,1,0:T(8,128)(2,1)}, u32[]{:S(2)}) copy-start(bf16[2,128,512]{2,1,0:T(8,128)(2,1)} %param.21) | copy-start | bytes 786436
  54.2 156.5 %reduce-scatter.2.cloned.1.call-start = ((), (), s32[]{:S(2)}) async-start(), calls=%async_computation.5 | async-start | bytes 4456448 | tf_op jit(solution)/shard_map/reduce_scatter | solution.py:113
  119.6 163.3 %all-gather.5.cloned.1.call-start = ((), (), s32[]{:S(2)}) async-start(), calls=%async_computation.6 | async-start | bytes 4456448 | tf_op jit(solution)/shard_map/all_gather | solution.py:107
  119.7 163.2 %copy-start.5 = (bf16[2,128,512]{2,1,0:T(8,128)(2,1)S(1)}, bf16[2,128,512]{2,1,0:T(8,128)(2,1)}, u32[]{:S(2)}) copy-start(bf16[2,128,512]{2,1,0:T(8,128)(2,1)} %param.25) | copy-start | bytes 786436
  119.7 163.2 %copy-start.6 = (bf16[2,128,512]{2,1,0:T(8,128)(2,1)S(1)}, bf16[2,128,512]{2,1,0:T(8,128)(2,1)}, u32[]{:S(2)}) copy-start(bf16[2,128,512]{2,1,0:T(8,128)(2,1)} %param.24) | copy-start | bytes 786436
  212.6 82.1 %all-to-all-start.1 = ((bf16[2,32,4,512]{3,2,0,1:T(4,128)(2,1)}), bf16[2,32,4,512]{3,2,0,1:T(4,128)(2,1)S(1)}, u32[]{:S(2)}, u32[]{:S(2)}) async-start(bf16[2,32,4,512]{3,2,0,1:T(4,128)(2,1)} %copy.31), calls=%async_computation.2 | async-start | bytes 524288 | tf_op jit(solution)/shard_map/all_to_all | solution.py:122
  294.7 1.0 copy-start.3
  294.7 1.5 copy-start.4
Sparse Core Ops, SparseCore 0:
  54.4 58.5 all-gather.2
  119.7 91.0 reduce-scatter.1
  214.8 68.0 all-gather.4
where the time goes:
time: 304 us; the launch traced here: 303 us
  waiting for transfers between devices  169 us (56%)
  blocking collectives  73.5 us (24%)
  matrix products  18.9 us (6%)
  starting transfers between devices  14.8 us (5%)
  between operations  14 us (5%)
  local copies, waits for them, and re-layouts  10 us (3%)
    all_gather x1, waiting for transfers between devices, local(): piece_x = lax.all_gather(recv_x, 'dp', axis=1, tiled=True)  58.6 us
    all_gather x1, waiting for transfers between devices, local(): piece_grad = lax.all_gather(recv_grad, 'dp', axis=1, tiled=True)  55.6 us
    reduce_scatter x1, waiting for transfers between devices, local(): lax.psum_scatter(jnp.einsum('rkf,kfd->rkd', hidden_all, w_down, preferred...  55.1 us
    all_to_all x1, blocking collectives, local(): lax.all_to_all(send_x, 'expert', split_axis=1, concat_axis=1, tiled=True)  38.5 us
    all_to_all x1, blocking collectives, local(): lax.all_to_all(send_grad, 'expert', split_axis=1, concat_axis=1, tiled=True)  34.9 us
    all_to_all x1, starting transfers between devices, local(): lax.all_to_all(outgoing, 'expert', split_axis=1, concat_axis=1, tiled=True)  14.6 us
    dot_general x1, matrix products, outer_in(): jnp.einsum('krd,krf->kdf', rows_x, hidden_grad, preferred_element_type=jn...  7.45 us
  transfers between devices with their start and end apart: 4, of which 3 were waited for; matrix products, arithmetic and copies ran while one was open for 5% of the time, Pallas kernels for 0%

commit v1 on v0

--- a/solution.py
+++ b/solution.py
@@ -103,7 +103,9 @@
     )
     recv_x = recv_x.reshape(local_count, recv_rows, width)
     recv_grad = recv_grad.reshape(local_count, recv_rows, width)
-    piece_x = lax.all_gather(recv_x, "dp", axis=1, tiled=True)
+    piece_x = jnp.concatenate(
+        lax.all_to_all(jnp.stack([recv_x] * lax.axis_size("dp")), "dp", 0, 0), axis=1
+    )
     piece_grad = lax.all_gather(recv_grad, "dp", axis=1, tiled=True)
     hidden, hidden_grad = expert_rows(piece_x, piece_grad, w_up, w_down)
     grad_in = outer_in(piece_x, hidden_grad)

time: 304 us -> 292 us (0.961)
  waiting for transfers between devices: 169 us -> 110 us
  blocking collectives: 73.5 us -> 123 us
    all_gather x1 -> x0, waiting for transfers between devices: 58.6 us -> none  [local(): piece_x = lax.all_gather(recv_x, 'dp', axis=1, tiled=True)]
    all_to_all x0 -> x1, blocking collectives: none -> 56.2 us  [local(): lax.all_to_all(jnp.stack([recv_x] * lax.axis_size('dp')), 'dp', 0, 0)]
    all_to_all x1, blocking collectives: 34.9 us -> 27.8 us  [local(): lax.all_to_all(send_grad, 'expert', split_axis=1, concat_axis=1, tiled=True)]
  transfers between devices with their start and end apart: 4 -> 3, of which waited for: 3 -> 2; matrix products, arithmetic and copies ran while one was open for 5% -> 5% of each run, Pallas kernels for 0% -> 0%
where the time goes in v1:
time: 292 us
  blocking collectives  123 us (42%)
  waiting for transfers between devices  110 us (38%)
  matrix products  16.8 us (6%)
  starting transfers between devices  14.8 us (5%)
  between operations  14.3 us (5%)
  local copies, waits for them, and re-layouts  11 us (4%)
    all_to_all x1, blocking collectives, local(): lax.all_to_all(jnp.stack([recv_x] * lax.axis_size('dp')), 'dp', 0, 0)  56.2 us
    all_gather x1, waiting for transfers between devices, local(): piece_grad = lax.all_gather(recv_grad, 'dp', axis=1, tiled=True)  55.6 us
    reduce_scatter x1, waiting for transfers between devices, local(): lax.psum_scatter(jnp.einsum('rkf,kfd->rkd', hidden_all, w_down, preferred...  54.3 us
    all_to_all x1, blocking collectives, local(): lax.all_to_all(send_x, 'expert', split_axis=1, concat_axis=1, tiled=True)  38.5 us
    all_to_all x1, blocking collectives, local(): lax.all_to_all(send_grad, 'expert', split_axis=1, concat_axis=1, tiled=True)  27.8 us
    all_to_all x1, starting transfers between devices, local(): lax.all_to_all(outgoing, 'expert', split_axis=1, concat_axis=1, tiled=True)  14.7 us
    dot_general x1, matrix products, outer_in(): jnp.einsum('krd,krf->kdf', rows_x, hidden_grad, preferred_element_type=jn...  7.45 us
  transfers between devices with their start and end apart: 3, of which 2 were waited for; matrix products, arithmetic and copies ran while one was open for 5% of the time, Pallas kernels for 0%

profile of v1, /device:TPU:1, one launch (start us, length us, event | category | flops | bytes accessed | tf_op | source)
XLA Modules:
  0.0 292.0 jit_solution(16573169113692655332)
XLA Ops:
  7.2 0.0 copy-start
  7.2 0.0 reduce-scatter.2.cloned.1.call-start
  7.2 0.8 select_reduce_fusion.2
  8.0 0.8 select_reduce_fusion.1
  8.8 0.1 fusion.28
  8.9 0.2 reduce_window_sum.11
  9.1 0.2 select_reduce_fusion
  9.3 1.0 scatter_custom_fusion
  10.3 0.9 concatenate.7
  11.3 0.9 concatenate.6
  12.2 1.2 gather_fusion.2
  13.3 1.2 gather_fusion.1
  14.5 0.1 broadcast_select_fusion
  14.6 0.1 reshape.146
  14.7 0.1 copy.39
  14.8 38.5 %all_to_all.20 = bf16[2,32,4,512]{3,2,0,1:T(4,128)(2,1)S(1)} all-to-all(bf16[2,32,4,512]{3,2,0,1:T(4,128)(2,1)S(1)} %copy.39), channel_id=1, replica_groups=mesh['dp'=16,'expert'=32] {'expert'}, dimensions={1} | all-to-all | bytes 524288 | tf_op jit(solution)/shard_map/all_to_all | solution.py:101
  53.3 0.2 copy.40
  53.6 0.5 stack.3
  54.0 56.2 %all_to_all.21 = bf16[16,2,128,512]{3,2,1,0:T(8,128)(2,1)S(1)} all-to-all(bf16[16,2,128,512]{3,2,1,0:T(8,128)(2,1)S(1)} %stack.3), channel_id=1, replica_groups=mesh['dp'=16,'expert'=32] {'dp'}, dimensions={0} | all-to-all | bytes 8388608 | tf_op jit(solution)/shard_map/all_to_all | solution.py:107
  110.3 0.4 copy.42
  110.7 0.0 copy-start.1
  110.7 0.5 copy-done.3
  111.2 1.3 fusion.46
  112.5 0.2 copy-done.1
  112.6 3.2 %convert_bitcast_fusion = bf16[2048,2,512]{2,0,1:T(8,128)(2,1)} fusion(bf16[2,128,512]{2,1,0:T(8,128)(2,1)S(1)} %copy-done.2, f32[2,2048,128]{2,1,0:T(8,128)S(1)} %fusion.46), kind=kOutput, calls=%fused_computation.4 | convolution fusion | flops 541589504 | bytes 6553600 | tf_op jit(solution)/shard_map/rkf,kfd->rkd/dot_general | solution.py:116
  115.9 0.0 reduce-scatter.2.cloned.1.call-update
  115.9 0.0 all-gather.2.cloned.1.call-start
  115.9 0.1 reshape.151
  116.0 0.0 copy-start.6
  116.0 0.0 copy-start.7
  116.0 0.1 copy.45
  116.1 27.8 %all_to_all.22 = bf16[2,32,4,512]{3,2,0,1:T(4,128)(2,1)S(1)} all-to-all(bf16[2,32,4,512]{3,2,0,1:T(4,128)(2,1)S(1)} %copy.45), channel_id=1, replica_groups=mesh['dp'=16,'expert'=32] {'expert'}, dimensions={1} | all-to-all | bytes 524288 | tf_op jit(solution)/shard_map/all_to_all | solution.py:102
  143.9 0.1 copy.46
  144.0 0.8 reshape.152
  144.8 0.0 all-gather.2.cloned.1.call-update
  144.8 54.3 %reduce-scatter.2.cloned.1.call-done = bf16[128,2,512]{2,0,1:T(8,128)(2,1)} async-done(((bf16[2048,2,512]{2,0,1:T(8,128)(2,1)}), bf16[128,2,512]{2,0,1:T(8,128)(2,1)}) %reduce-scatter.2.cloned.1.call-update) | async-done | bytes 262160 | tf_op jit(solution)/shard_map/reduce_scatter | solution.py:115
  199.1 1.0 reshape.149
  200.1 0.8 copy.43
  200.9 14.7 %all-to-all-start.2 = ((bf16[2,32,4,512]{3,2,0,1:T(4,128)(2,1)}), bf16[2,32,4,512]{3,2,0,1:T(4,128)(2,1)S(1)}, u32[]{:S(2)}, u32[]{:S(2)}) async-start(bf16[2,32,4,512]{3,2,0,1:T(4,128)(2,1)} %copy.43), calls=%async_computation.3 | async-start | bytes 524288 | tf_op jit(solution)/shard_map/all_to_all | solution.py:124
  215.6 55.6 %all-gather.2.cloned.1.call-done = bf16[2,2048,512]{2,1,0:T(8,128)(2,1)} async-done(((bf16[2,128,512]{2,1,0:T(8,128)(2,1)}), bf16[2,2048,512]{2,1,0:T(8,128)(2,1)}) %all-gather.2.cloned.1.call-update) | async-done | bytes 4194320 | tf_op jit(solution)/shard_map/all_gather | solution.py:109
  271.2 4.4 %fusion.19 = (bf16[2,128,512]{2,1,0:T(8,128)(2,1)}, bf16[2,128,512]{2,1,0:T(8,128)(2,1)}, bf16[2,128,512]{2,1,0:T(8,128)(2,1)}) fusion(bf16[2,128,512]{2,1,0:T(8,128)(2,1)S(1)} %copy-done.6, bf16[2,128,512]{2,1,0:T(8,128)(2,1)S(1)} %copy-done.7, bf16[2,128,512]{2,1,0:T(8,128)(2,1)S(1)} %copy-done.2, bf16[2,2048,512]{2,1,0:T(8,128)(2,1)} %all-gather.2.cloned.1.call-done, ...), kind=kOutput, calls=%fused_computation.35 | convolution fusion | flops 541982720 | bytes 7864320 | tf_op jit(solution)/shard_map/krf,krd->kfd/dot_general | solution.py:71
  275.6 7.5 %fusion.20 = (bf16[2,512,128]{2,1,0:T(8,128)(2,1)}, bf16[2,512,128]{2,1,0:T(8,128)(2,1)}, bf16[2,512,128]{2,1,0:T(8,128)(2,1)}) fusion(bf16[2,512,128]{2,1,0:T(8,128)(2,1)} %param.23, bf16[2,512,128]{2,1,0:T(8,128)(2,1)} %param.22, bf16[2,512,128]{2,1,0:T(8,128)(2,1)S(1)} %copy-done.3, bf16[2,2048,512]{2,1,0:T(8,128)(2,1)} %bitcast.51, ...), kind=kOutput, calls=%fused_computation.36 | convolution fusion | flops 1081475072 | bytes 12320768 | tf_op jit(solution)/shard_map/krd,krf->kdf/dot_general | solution.py:67
  283.0 0.0 all-to-all-done.2
  283.0 0.1 copy.44
  283.1 0.1 reshape.150
  283.2 0.8 gather_fusion
  284.1 0.5 fusion.45
  284.5 0.6 multiply_divide_fusion
  (18 shorter events, 0.1 us)
Async XLA Ops:
  7.2 276.9 %copy-start = (f32[512,16]{0,1:T(8,128)S(1)}, f32[512,16]{0,1:T(8,128)}, u32[]{:S(2)}) copy-start(f32[512,16]{0,1:T(8,128)} %param.19) | copy-start | bytes 98308
  7.2 191.9 %reduce-scatter.2.cloned.1.call-start = ((), (), s32[]{:S(2)}) async-start(), calls=%async_computation.5 | async-start | bytes 4456448 | tf_op jit(solution)/shard_map/reduce_scatter | solution.py:115
  110.3 1.0 copy-start.3
  110.7 1.9 copy-start.1
  111.2 1.4 copy-start.2
  115.9 155.3 %all-gather.2.cloned.1.call-start = ((), (), s32[]{:S(2)}) async-start(), calls=%async_computation.6 | async-start | bytes 4456448 | tf_op jit(solution)/shard_map/all_gather | solution.py:109
  116.0 155.2 %copy-start.6 = (bf16[2,128,512]{2,1,0:T(8,128)(2,1)S(1)}, bf16[2,128,512]{2,1,0:T(8,128)(2,1)}, u32[]{:S(2)}) copy-start(bf16[2,128,512]{2,1,0:T(8,128)(2,1)} %param.25) | copy-start | bytes 786436
  116.0 155.2 %copy-start.7 = (bf16[2,128,512]{2,1,0:T(8,128)(2,1)S(1)}, bf16[2,128,512]{2,1,0:T(8,128)(2,1)}, u32[]{:S(2)}) copy-start(bf16[2,128,512]{2,1,0:T(8,128)(2,1)} %param.24) | copy-start | bytes 786436
  200.9 82.1 %all-to-all-start.2 = ((bf16[2,32,4,512]{3,2,0,1:T(4,128)(2,1)}), bf16[2,32,4,512]{3,2,0,1:T(4,128)(2,1)S(1)}, u32[]{:S(2)}, u32[]{:S(2)}) async-start(bf16[2,32,4,512]{3,2,0,1:T(4,128)(2,1)} %copy.43), calls=%async_computation.3 | async-start | bytes 524288 | tf_op jit(solution)/shard_map/all_to_all | solution.py:124
  283.0 1.0 copy-start.4
  283.0 1.5 copy-start.5
Sparse Core Ops, SparseCore 0:
  116.0 83.0 reduce-scatter.1
  203.1 68.0 all-gather.1
